TPU v7x, 32 devices: a whole 2x2x4 slice. The times are simulated.
32 devices in a mesh: beam: 4 (over x, core), depth: 8 (over z, y).
Axes of the slice: x: 2, y: 2, z: 4, core: 2. Of those that a mesh axis runs over, the one named last changes fastest.
Arguments:
- concentration: float32 [128, 1024, 256], P('beam', 'depth'), may hold values from 0.25 to 2.5
- entry_intensity: float32 [1024, 256], P('depth'), may hold values from 0.25 to 1.75
- absorb: float32 [256], replicated, may hold values from 0.0015625 to 0.01953125
- blur_taps: float32 [5], replicated, may hold values from 0.1 to 1
- measured: float32 [128, 256], P('beam'), may hold values from -6 to 6
Outputs:
- descent: float32 [128, 1024, 256], P('beam', 'depth')
- residual: float32 [128, 256], P('beam', 'depth')
All inputs are finite; a program needn't handle non-finite values.
Results may differ from a plain program's by a relative error of at most 0.000058.
Values sent between devices are 32-bit elements; how exact they have to be, the bound alone decides.
A program may use at most 64 MiB of HBM per device.

v0:
```python
import jax
import jax.numpy as jnp
from jax import lax
from jax.sharding import PartitionSpec as P


def entering(x, axis, combine, identity, reverse):
    devices, index = (lax.axis_size(axis), lax.axis_index(axis))
    everything = lax.all_gather(x, axis)
    start = jnp.broadcast_to(jnp.asarray(identity, x.dtype), x.shape)

    def lap(k, before):
        at = devices - 1 - k if reverse else k
        reached = at > index if reverse else at < index
        new = combine(before, everything[at])
        return jnp.where(reached, new, before)

    return lax.fori_loop(0, devices, lap, start)


def blur_rows(padded, blur_taps, width):
    total = blur_taps[0] * padded[:, 0:width]
    for k in range(1, 5):
        total = total + blur_taps[k] * padded[:, k : k + width]
    return total


def adjoint_rows(padded, blur_taps, width):
    total = blur_taps[0] * padded[:, 4 : 4 + width]
    for k in range(1, 5):
        total = total + blur_taps[k] * padded[:, 4 - k : 4 - k + width]
    return total


def local(concentration, entry_intensity, absorb, blur_taps, measured):
    cells_beam, cells_depth, height = concentration.shape
    depth_count = lax.axis_size("depth")
    scale = 1.0 / (cells_depth * depth_count)
    row_ids = lax.broadcasted_iota(jnp.int32, (cells_beam, cells_beam), 0)
    col_ids = lax.broadcasted_iota(jnp.int32, (cells_beam, cells_beam), 1)
    lower = (col_ids < row_ids).astype(jnp.float32)
    upper = (col_ids > row_ids).astype(jnp.float32)
    local_prior = jnp.einsum("ab,bdh->adh", lower, concentration, precision=lax.Precision.HIGHEST)
    totals = jnp.sum(concentration, axis=0)
    before = entering(totals, "beam", jnp.add, jnp.zeros_like(totals), False)
    lit = entry_intensity[None] * jnp.exp(-absorb * (before[None] + local_prior))
    partial_value = jnp.sum(lit * concentration, axis=1)
    width = height // depth_count
    section_start = lax.axis_index("depth") * width
    whole = lax.psum(partial_value, "depth") * scale
    predicted = blur_rows(jnp.pad(whole, ((0, 0), (2, 2))), blur_taps, height)
    full_residual = predicted - measured
    residual = lax.dynamic_slice_in_dim(full_residual, section_start, width, 1)
    back = adjoint_rows(jnp.pad(full_residual, ((0, 0), (2, 2))), blur_taps, height)
    q_term = back[:, None, :] * lit
    weighted = q_term * concentration
    local_later = jnp.einsum("ab,bdh->adh", upper, weighted, precision=lax.Precision.HIGHEST)
    weight_totals = jnp.sum(weighted, axis=0)
    after = entering(weight_totals, "beam", jnp.add, jnp.zeros_like(weight_totals), True)
    descent = absorb * (after[None] + local_later) - q_term
    return (descent, residual)


def solution(mesh):
    return jax.shard_map(
        local,
        mesh=mesh,
        in_specs=(P("beam", "depth", None), P("depth", None), P(), P(), P("beam", None)),
        out_specs=(P("beam", "depth", None), P("beam", "depth")),
        check_vma=False,
    )
```

profile of v0, /device:TPU:0, one launch (start us, length us, event | category | flops | bytes accessed | tf_op | source)
XLA Modules:
  0.0 100.8 jit_solution(4324508441356175733)
XLA Ops:
  0.6 0.0 copy-start
  0.6 0.7 neg.3
  1.4 1.5 %fusion.27 = (f32[1]{0:T(128)}, f32[1]{0:T(128)}, f32[1]{0:T(128)}, f32[1]{0:T(128)}, f32[1]{0:T(128)}) fusion(f32[5]{0:T(128)} %param.12), kind=kLoop, calls=%fused_computation.43 | loop fusion | bytes 40 | tf_op jit(solution)/shard_map/slice | solution.py:29
  3.5 2.5 %reduce_sum.27 = f32[128,256]{1,0:T(8,128)S(1)} reduce(f32[32,128,256]{2,1,0:T(8,128)} %param.9, f32[]{:T(128)} %constant.78.clone.1), dimensions={0}, to_apply=%region_0.0 | reduce | flops 1015808 | bytes 4325380 | tf_op jit(solution)/shard_map/reduce_sum | solution.py:44
  6.0 8.6 %all-gather = f32[512,256]{1,0:T(8,128)S(1)} all-gather(f32[128,256]{1,0:T(8,128)S(1)} %reduce_sum.27), channel_id=2, replica_groups=mesh['beam'=4,'depth'=8] {'beam'}, dimensions={0}, use_global_device_ids=true | all-gather | bytes 655360 | tf_op jit(solution)/shard_map/all_gather | solution.py:9
  14.6 0.2 while.30
  14.8 0.0 copy-done
  14.8 0.0 copy-start.1
  14.8 12.4 %multiply_reduce_fusion = (f32[32,256]{1,0:T(8,128)S(1)}, f32[32,128,256]{2,0,1:T(8,128)}) fusion(f32[32,128,256]{2,1,0:T(8,128)} %param.9, f32[128,256]{1,0:T(8,128)S(1)} %get-tuple-element.191, f32[256]{0:T(256)S(1)} %neg.3, f32[128,256]{1,0:T(8,128)S(1)} %copy-done), kind=kOutput, calls=%fused_computation.3 | convolution fusion | flops 407888896 | bytes 8684544 | tf_op jit(solution)/shard_map/ab,bdh->adh/dot_general | solution.py:43
  27.2 37.4 %psum.7 = f32[32,256]{1,0:T(8,128)S(1)} all-reduce(f32[32,256]{1,0:T(8,128)S(1)} %get-tuple-element.246), channel_id=1, replica_groups=mesh['beam'=4,'depth'=8] {'depth'}, use_global_device_ids=true, to_apply=%region_4.5 | all-reduce | flops 8192 | bytes 65536 | tf_op jit(solution)/shard_map/psum | solution.py:50
  64.6 0.0 copy-done.1
  64.7 2.5 %fusion.11 = f32[32,256]{1,0:T(8,128)S(1)} fusion(f32[32,256]{1,0:T(8,128)S(1)} %copy-done.1, f32[32,256]{1,0:T(8,128)S(1)} %broadcast_multiply_fusion, f32[32,256]{1,0:T(8,128)S(1)} %psum.7, f32[]{:T(128)} %bitcast.6, f32[]{:T(128)} %bitcast.5, f32[]{:T(128)S(6)} %mul.113, f32[]{:T(128)} %bitcast.3, f32[]{:T(128)} %bitcast), kind=kLoop, calls=%fused_computation.25 | loop fusion | flops 81920 | bytes 131092 | tf_op jit(solution)/shard_map/sub | solution.py:52
  67.2 0.7 constant_dynamic-slice_fusion
  67.9 3.1 %fusion.19 = f32[32,256]{1,0:T(8,128)S(1)} fusion(f32[32,256]{1,0:T(8,128)S(1)} %fusion.11, f32[]{:T(128)} %bitcast.4, f32[]{:T(128)} %bitcast.6, f32[]{:T(128)} %bitcast.5, f32[]{:T(128)} %bitcast.3, f32[]{:T(128)} %bitcast), kind=kLoop, calls=%fused_computation.33 | loop fusion | flops 73728 | bytes 65556 | tf_op jit(solution)/shard_map/add | solution.py:31
  71.0 0.0 copy-start.2
  71.0 6.8 %fusion.2 = f32[128,256]{1,0:T(8,128)S(1)} fusion(f32[32,128,256]{2,1,0:T(8,128)} %param.9, f32[32,128,256]{2,0,1:T(8,128)} %get-tuple-element.247, f32[32,256]{1,0:T(8,128)S(1)} %fusion.19, f32[128,256]{1,0:T(8,128)S(1)} %get-tuple-element.191, f32[256]{0:T(256)S(1)} %neg.3, f32[128,256]{1,0:T(8,128)S(1)} %copy-done), kind=kLoop, calls=%fused_computation.8 | loop fusion | flops 6258688 | bytes 8815616 | tf_op jit(solution)/shard_map/reduce_sum | solution.py:58
  77.8 7.0 %all-gather.1 = f32[512,256]{1,0:T(8,128)S(1)} all-gather(f32[128,256]{1,0:T(8,128)S(1)} %fusion.2), channel_id=3, replica_groups=mesh['beam'=4,'depth'=8] {'beam'}, dimensions={0}, use_global_device_ids=true | all-gather | bytes 655360 | tf_op jit(solution)/shard_map/all_gather | solution.py:9
  84.8 0.3 while.31
  85.1 0.0 copy-done.2
  85.1 11.2 %multiply_subtract_fusion = f32[32,128,256]{2,0,1:T(8,128)S(1)} fusion(f32[32,128,256]{2,0,1:T(8,128)} %get-tuple-element.247, f32[128,256]{1,0:T(8,128)S(1)} %get-tuple-element.192, f32[32,256]{1,0:T(8,128)S(1)} %fusion.19, f32[32,128,256]{2,1,0:T(8,128)} %param.9, f32[128,256]{1,0:T(8,128)S(1)} %get-tuple-element.191, f32[256]{0:T(256)S(1)} %neg.3, ...), kind=kOutput, calls=%fused_computation.2 | convolution fusion | flops 415237120 | bytes 13010944 | tf_op jit(solution)/shard_map/ab,bdh->adh/dot_general | solution.py:57
  96.3 4.4 %copy.10 = f32[32,128,256]{2,1,0:T(8,128)} copy(f32[32,128,256]{2,0,1:T(8,128)S(1)} %multiply_subtract_fusion) | data formatting | bytes 8388608
  (11 shorter events, 0.3 us)
Async XLA Ops:
  0.6 14.2 %copy-start = (f32[128,256]{1,0:T(8,128)S(1)}, f32[128,256]{1,0:T(8,128)}, u32[]{:S(2)}) copy-start(f32[128,256]{1,0:T(8,128)} %param.10) | copy-start | bytes 393220
  14.8 49.8 %copy-start.1 = (f32[32,256]{1,0:T(8,128)S(1)}, f32[32,256]{1,0:T(8,128)}, u32[]{:S(2)}) copy-start(f32[32,256]{1,0:T(8,128)} %param.13) | copy-start | bytes 98308
  71.0 14.1 %copy-start.2 = (f32[256]{0:T(256)S(1)}, f32[256]{0:T(256)}, u32[]{:S(2)}) copy-start(f32[256]{0:T(256)} %param.11) | copy-start | bytes 3076
where the time goes:
time: 101 us
  blocking collectives  53 us (52%)
  matrix products  23.6 us (23%)
  other arithmetic  16 us (16%)
  local copies, waits for them, and re-layouts  6.63 us (7%)
  between operations  1.38 us (1%)
    psum x1, blocking collectives, local(): whole = lax.psum(partial_value, 'depth') * scale  37.4 us
    all_gather x2, blocking collectives, entering(): everything = lax.all_gather(x, axis)  15.6 us
    dot_general x1, matrix products, local(): jnp.einsum('ab,bdh->adh', lower, concentration, precision=lax.Precision.H...  12.4 us
    dot_general x1, matrix products, local(): jnp.einsum('ab,bdh->adh', upper, weighted, precision=lax.Precision.HIGHEST)  11.2 us
    reduce_sum x1, other arithmetic, local(): weight_totals = jnp.sum(weighted, axis=0)  6.82 us
    unnamed x7, local copies, waits for them, and re-layouts  4.46 us
    add x1, other arithmetic, adjoint_rows(): total = total + blur_taps[k] * padded[:, 4 - k:4 - k + width]  3.14 us
    sub x1, other arithmetic, local(): full_residual = predicted - measured  2.51 us

commit v1 on v0

v1 whole, which is shorter than its diff:
```python
import functools

import jax
import jax.numpy as jnp
from jax import lax
from jax.experimental import pallas as pl
from jax.experimental.pallas import tpu as pltpu
from jax.sharding import PartitionSpec as P

MESH = pl.DeviceIdType.MESH
ROWS, LANES = 8, 128
CHUNKS = 4


def blur(x, taps, sign):
    width = x.shape[1]
    lane = lax.broadcasted_iota(jnp.int32, x.shape, 1)
    total = jnp.zeros_like(x)
    for k in range(5):
        step = sign * (k - 2)
        moved = x if step == 0 else pltpu.roll(x, (-step) % width, 1)
        inside = (lane + step >= 0) & (lane + step < width)
        total = total + taps[k] * jnp.where(inside, moved, 0.0)
    return total


def exchange_kernel(
    nb, nd, c_hbm, entry, absorb, taps_ref, measured,
    light_out, back_out, after_out, res_out,
    w, tot, pbuf, ps, qbuf, fs, fbuf, before, img, rs, ag,
    load_sem, a_send, a_recv, b_send, b_recv, f_send, f_recv,
    rs_send, rs_recv, ag_send, ag_recv,
):
    cells, depth, height = w.shape
    half = depth // 2
    pairs = nb // 2
    bi = lax.axis_index("beam")
    di = lax.axis_index("depth")
    core = lax.rem(bi, 2)
    pair = bi // 2
    partner = bi + 1 - 2 * core
    tiles = depth // ROWS
    lane_blocks = height // LANES
    pieces = (cells // ROWS) * lane_blocks
    owners = min(nd, pieces)
    per = pieces // owners

    step = depth // CHUNKS
    loads = []
    for k in range(CHUNKS):
        part = pl.ds(k * step, step)
        copy = pltpu.make_async_copy(c_hbm.at[:, part, :], w.at[:, part, :], load_sem.at[k])
        copy.start()
        loads.append(copy)

    barrier = pltpu.get_barrier_semaphore()
    for k in range(1, nb):
        pl.semaphore_signal(
            barrier, inc=1, device_id={"beam": lax.rem(bi + k, nb)}, device_id_type=MESH
        )
    for k in range(1, nd):
        pl.semaphore_signal(
            barrier, inc=1, device_id={"depth": lax.rem(di + k, nd)}, device_id_type=MESH
        )

    def totals(i, carry):
        rows = pl.ds(pl.multiple_of(i * ROWS, ROWS), ROWS)
        parts = [w[b, rows, :] for b in range(4)]
        for b in range(4, cells):
            parts[b % 4] = parts[b % 4] + w[b, rows, :]
        tot[0, rows, :] = (parts[0] + parts[1]) + (parts[2] + parts[3])
        return carry

    for k in range(CHUNKS):
        loads[k].wait()
        lax.fori_loop(k * step // ROWS, (k + 1) * step // ROWS, totals, 0)

    pl.semaphore_wait(barrier, nb - 1 + nd - 1)

    own_rows = pl.ds(pl.multiple_of(core * half, ROWS), half)
    other_rows = pl.ds(pl.multiple_of((1 - core) * half, ROWS), half)

    def to_partner(ph, slot):
        return pltpu.make_async_remote_copy(
            src_ref=tot.at[ph, other_rows if slot == 0 else own_rows, :],
            dst_ref=pbuf.at[ph, slot],
            send_sem=a_send.at[ph, slot],
            recv_sem=a_recv.at[ph, slot],
            device_id={"beam": partner},
            device_id_type=MESH,
        )

    def to_pair(ph, target):
        return pltpu.make_async_remote_copy(
            src_ref=ps.at[ph],
            dst_ref=qbuf.at[ph, pair],
            send_sem=b_send.at[ph, target],
            recv_sem=b_recv.at[ph, pair],
            device_id={"beam": 2 * target + core},
            device_id_type=MESH,
        )

    def from_pair(ph, source):
        return pltpu.make_async_remote_copy(
            src_ref=ps.at[ph],
            dst_ref=qbuf.at[ph, source],
            send_sem=b_send.at[ph, source],
            recv_sem=b_recv.at[ph, source],
            device_id={"beam": 2 * source + core},
            device_id_type=MESH,
        )

    def forward(ph):
        return pltpu.make_async_remote_copy(
            src_ref=fs.at[ph],
            dst_ref=fbuf.at[ph],
            send_sem=f_send.at[ph],
            recv_sem=f_recv.at[ph],
            device_id={"beam": partner},
            device_id_type=MESH,
        )

    def downstream(ph, other):
        return other > pair if ph == 0 else other < pair

    def upstream(ph, other):
        return other < pair if ph == 0 else other > pair

    def exchange_begin(ph):
        to_partner(ph, 0).start()
        to_partner(ph, 1).start()
        to_partner(ph, 0).wait_recv()
        if pairs > 1:
            ps[ph] = tot[ph, own_rows, :] + pbuf[ph, 0]
            for target in range(pairs):
                @pl.when(downstream(ph, target))
                def _():
                    to_pair(ph, target).start()

    def exchange_end(ph, result):
        to_partner(ph, 1).wait_recv()
        takes = core == (1 if ph == 0 else 0)

        @pl.when(takes)
        def _():
            result[own_rows, :] = pbuf[ph, 0]
            result[other_rows, :] = pbuf[ph, 1]

        @pl.when(jnp.logical_not(takes))
        def _():
            result[...] = jnp.zeros_like(result)

        if pairs > 1:
            first = 0 if ph == 0 else pairs - 1

            @pl.when(upstream(ph, first))
            def _():
                from_pair(ph, first).wait_recv()
                fs[ph] = qbuf[ph, first]
                for source in range(pairs):
                    if source != first:
                        @pl.when(upstream(ph, source))
                        def _():
                            from_pair(ph, source).wait_recv()
                            fs[ph] = fs[ph] + qbuf[ph, source]
                forward(ph).start()
                result[own_rows, :] = result[own_rows, :] + fs[ph]
                forward(ph).wait_recv()
                result[other_rows, :] = result[other_rows, :] + fbuf[ph]

    def exchange_sent(ph):
        to_partner(ph, 0).wait_send()
        to_partner(ph, 1).wait_send()
        if pairs > 1:
            for target in range(pairs):
                @pl.when(downstream(ph, target))
                def _():
                    to_pair(ph, target).wait_send()

            @pl.when(upstream(ph, 0 if ph == 0 else pairs - 1))
            def _():
                forward(ph).wait_send()

    exchange_begin(0)

    def weigh(i, carry):
        rows = pl.ds(pl.multiple_of(i * ROWS, ROWS), ROWS)
        for j in range(lane_blocks):
            lanes = pl.ds(j * LANES, LANES)
            rate = -absorb[:, lanes]
            prior = w[0, rows, lanes]
            for b in range(1, cells):
                c = w[b, rows, lanes]
                w[b, rows, lanes] = c * jnp.exp(rate * prior)
                prior = prior + c
        return carry

    lax.fori_loop(0, tiles, weigh, 0)

    exchange_end(0, before)
    light_out[...] = entry[...] * jnp.exp(-absorb[...] * before[...])

    def emit(g, carry):
        for j in range(lane_blocks):
            lanes = pl.ds(j * LANES, LANES)
            sums = []
            for r in range(ROWS):
                acc = [None, None]
                for t in range(tiles):
                    rows = pl.ds(t * ROWS, ROWS)
                    term = light_out[rows, lanes] * w[g * ROWS + r, rows, lanes]
                    acc[t % 2] = term if acc[t % 2] is None else acc[t % 2] + term
                sums.append(jnp.sum(acc[0] + acc[1], axis=0, keepdims=True))
            img[g * lane_blocks + j] = jnp.concatenate(sums, axis=0)
        return carry

    lax.fori_loop(0, cells // ROWS, emit, 0)

    def guarded(index, body):
        if owners == nd:
            body()
        else:
            pl.when(index < owners)(body)

    def scatter(target, k):
        return pltpu.make_async_remote_copy(
            src_ref=img.at[pl.ds(target * per, per)],
            dst_ref=rs.at[di],
            send_sem=rs_send.at[k],
            recv_sem=rs_recv.at[di],
            device_id={"depth": target},
            device_id_type=MESH,
        )

    def scattered(source, k):
        return pltpu.make_async_remote_copy(
            src_ref=img.at[pl.ds(0, per)],
            dst_ref=rs.at[source],
            send_sem=rs_send.at[k],
            recv_sem=rs_recv.at[source],
            device_id={"depth": source},
            device_id_type=MESH,
        )

    def gather(target, k):
        mine = pl.ds(di * per, per)
        return pltpu.make_async_remote_copy(
            src_ref=ag.at[mine],
            dst_ref=ag.at[mine],
            send_sem=ag_send.at[k],
            recv_sem=ag_recv.at[di],
            device_id={"depth": target},
            device_id_type=MESH,
        )

    def gathered(source, k):
        theirs = pl.ds(source * per, per)
        return pltpu.make_async_remote_copy(
            src_ref=ag.at[theirs],
            dst_ref=ag.at[theirs],
            send_sem=ag_send.at[k],
            recv_sem=ag_recv.at[source],
            device_id={"depth": source},
            device_id_type=MESH,
        )

    for k in range(1, nd):
        target = lax.rem(di + k, nd)
        guarded(target, lambda target=target, k=k: scatter(target, k).start())

    def reduce_own():
        total = img[pl.ds(di * per, per)]
        for k in range(1, nd):
            source = lax.rem(di + k, nd)
            scattered(source, k).wait_recv()
            total = total + rs[source]
        ag[pl.ds(di * per, per)] = total * (1.0 / (depth * nd))
        for k in range(1, nd):
            gather(lax.rem(di + k, nd), k).start()

    guarded(di, reduce_own)

    for k in range(1, nd):
        source = lax.rem(di + k, nd)
        guarded(source, lambda source=source, k=k: gathered(source, k).wait_recv())

    image = jnp.concatenate(
        [
            jnp.concatenate([ag[g * lane_blocks + j] for j in range(lane_blocks)], axis=1)
            for g in range(cells // ROWS)
        ],
        axis=0,
    )
    taps = [taps_ref[k] for k in range(5)]
    residual = blur(image, taps, 1) - measured[...]
    res_out[...] = residual
    back_out[...] = blur(residual, taps, -1)

    def weighted(i, carry):
        rows = pl.ds(pl.multiple_of(i * ROWS, ROWS), ROWS)
        parts = [back_out[b:b + 1, :] * w[b, rows, :] for b in range(4)]
        for b in range(4, cells):
            parts[b % 4] = parts[b % 4] + back_out[b:b + 1, :] * w[b, rows, :]
        tot[1, rows, :] = light_out[rows, :] * ((parts[0] + parts[1]) + (parts[2] + parts[3]))
        return carry

    lax.fori_loop(0, tiles, weighted, 0)
    exchange_begin(1)
    exchange_end(1, after_out)

    exchange_sent(0)
    exchange_sent(1)
    for k in range(1, nd):
        target = lax.rem(di + k, nd)
        guarded(target, lambda target=target, k=k: scatter(target, k).wait_send())

    def sent():
        for k in range(1, nd):
            gather(lax.rem(di + k, nd), k).wait_send()

    guarded(di, sent)


def exchange(nb, nd, concentration, entry, absorb, taps, measured):
    cells, depth, height = concentration.shape
    half, pairs = depth // 2, nb // 2
    pieces = (cells // ROWS) * (height // LANES)
    per = pieces // min(nd, pieces)
    f32 = jnp.float32
    dma = pltpu.SemaphoreType.DMA
    vmem = pl.BlockSpec(memory_space=pltpu.VMEM)
    return pl.pallas_call(
        functools.partial(exchange_kernel, nb, nd),
        out_shape=[
            jax.ShapeDtypeStruct((depth, height), f32),
            jax.ShapeDtypeStruct((cells, height), f32),
            jax.ShapeDtypeStruct((depth, height), f32),
            jax.ShapeDtypeStruct((cells, height), f32),
        ],
        in_specs=[
            pl.BlockSpec(memory_space=pl.ANY), vmem, vmem,
            pl.BlockSpec(memory_space=pltpu.SMEM), vmem,
        ],
        out_specs=[vmem] * 4,
        scratch_shapes=[
            pltpu.VMEM((cells, depth, height), f32),
            pltpu.VMEM((2, depth, height), f32),
            pltpu.VMEM((2, 2, half, height), f32),
            pltpu.VMEM((2, half, height), f32),
            pltpu.VMEM((2, pairs, half, height), f32),
            pltpu.VMEM((2, half, height), f32),
            pltpu.VMEM((2, half, height), f32),
            pltpu.VMEM((depth, height), f32),
            pltpu.VMEM((pieces, ROWS, LANES), f32),
            pltpu.VMEM((nd, per, ROWS, LANES), f32),
            pltpu.VMEM((pieces, ROWS, LANES), f32),
            dma((CHUNKS,)), dma((2, 2)), dma((2, 2)),
            dma((2, pairs)), dma((2, pairs)), dma((2,)), dma((2,)),
            dma((nd,)), dma((nd,)), dma((nd,)), dma((nd,)),
        ],
        compiler_params=pltpu.CompilerParams(
            collective_id=0, has_side_effects=True, vmem_limit_bytes=24 * 2**20
        ),
        name="exchange",
    )(concentration, entry, absorb, taps, measured)


def descent_kernel(nd, c_ref, light_ref, after_ref, back_ref, absorb_ref, res_ref, out_ref, res_out):
    cells, depth, height = c_ref.shape
    width = height // nd

    @pl.when(pl.program_id(0) == 0)
    def _():
        di = lax.axis_index("depth")
        for k in range(nd):
            @pl.when(di == k)
            def _():
                res_out[...] = res_ref[:, k * width:(k + 1) * width]

    def tile(i, carry):
        rows = pl.ds(pl.multiple_of(i * ROWS, ROWS), ROWS)
        for j in range(height // LANES):
            lanes = pl.ds(j * LANES, LANES)
            rate = absorb_ref[:, lanes]
            light = light_ref[rows, lanes]
            prior = None
            q = []
            for b in range(cells):
                trans = light if prior is None else light * jnp.exp(-rate * prior)
                q.append(back_ref[b:b + 1, lanes] * trans)
                c = c_ref[b, rows, lanes]
                prior = c if prior is None else prior + c
            later = after_ref[rows, lanes]
            for b in reversed(range(cells)):
                out_ref[b, rows, lanes] = rate * later - q[b]
                later = later + q[b] * c_ref[b, rows, lanes]
        return carry

    lax.fori_loop(0, depth // ROWS, tile, 0)


def write_descent(nd, concentration, light, after, back, absorb, residual):
    cells, depth, height = concentration.shape
    block = 2 * ROWS
    big = pl.BlockSpec((cells, block, height), lambda i: (0, i, 0))
    flat = pl.BlockSpec((block, height), lambda i: (i, 0))
    whole = lambda shape: pl.BlockSpec(shape, lambda i: (0, 0))
    return pl.pallas_call(
        functools.partial(descent_kernel, nd),
        grid=(depth // block,),
        out_shape=[
            jax.ShapeDtypeStruct(concentration.shape, jnp.float32),
            jax.ShapeDtypeStruct((cells, height // nd), jnp.float32),
        ],
        in_specs=[big, flat, flat, whole(back.shape), whole(absorb.shape), whole(residual.shape)],
        out_specs=[big, whole((cells, height // nd))],
        compiler_params=pltpu.CompilerParams(vmem_limit_bytes=24 * 2**20),
        name="descent",
    )(concentration, light, after, back, absorb, residual)


def solution(mesh):
    nb, nd = mesh.shape["beam"], mesh.shape["depth"]

    def local(concentration, entry_intensity, absorb, blur_taps, measured):
        absorb = absorb.reshape(1, -1)
        light, back, after, residual = exchange(
            nb, nd, concentration, entry_intensity, absorb, blur_taps, measured
        )
        return tuple(write_descent(nd, concentration, light, after, back, absorb, residual))

    return jax.shard_map(
        local,
        mesh=mesh,
        in_specs=(P("beam", "depth", None), P("depth", None), P(), P(), P("beam", None)),
        out_specs=(P("beam", "depth", None), P("beam", "depth")),
        check_vma=False,
    )
```

time: 101 us -> 37 us (0.37)
  blocking collectives: 53 us -> 0 us
  Pallas kernels: 0 us -> 30.9 us
  matrix products: 23.6 us -> 0 us
  other arithmetic: 16 us -> 0 us
  local copies, waits for them, and re-layouts: 6.63 us -> 5.18 us
    psum x1 -> x0, blocking collectives: 37.4 us -> none  [local(): whole = lax.psum(partial_value, 'depth') * scale]
    pallas_call x0 -> x2, Pallas kernels: none -> 30.9 us  [the longest x1 26.4 us: exchange(): pl.pallas_call(functools.partial(exchange_kernel, nb, nd), out_shape=[jax...]
    dot_general x2 -> x0, matrix products: 23.6 us -> none  [the longest x1 12.4 us: local(): jnp.einsum('ab,bdh->adh', lower, concentration, precision=lax.Precision.H...]
    all_gather x2 -> x0, blocking collectives: 15.6 us -> none  [entering(): everything = lax.all_gather(x, axis)]
    reduce_sum x2 -> x0, other arithmetic: 9.28 us -> none  [the longest x1 6.82 us: local(): weight_totals = jnp.sum(weighted, axis=0)]
    add x1 -> x0, other arithmetic: 3.14 us -> none  [adjoint_rows(): total = total + blur_taps[k] * padded[:, 4 - k:4 - k + width]]
    sub x1 -> x0, other arithmetic: 2.51 us -> none  [local(): full_residual = predicted - measured]
    slice x1 -> x0, local copies, waits for them, and re-layouts: 1.49 us -> none  [adjoint_rows(): total = blur_taps[0] * padded[:, 4:4 + width]]
where the time goes in v1:
time: 37 us; the launch traced here: 36.8 us
  Pallas kernels  30.9 us (84%)
  local copies, waits for them, and re-layouts  5.18 us (14%)
  between operations  0.65 us (2%)
    pallas_call x1, Pallas kernels, exchange(): pl.pallas_call(functools.partial(exchange_kernel, nb, nd), out_shape=[jax...  26.4 us
    unnamed x10, local copies, waits for them, and re-layouts  5.18 us
    pallas_call x1, Pallas kernels, write_descent(): pl.pallas_call(functools.partial(descent_kernel, nd), grid=(depth // bloc...  4.5 us

profile of v1, /device:TPU:0, one launch (start us, length us, event | category | flops | bytes accessed | tf_op | source)
XLA Modules:
  0.0 36.8 jit_solution(12654605483498060455)
XLA Ops:
  0.6 0.0 copy-start
  0.6 2.2 %copy-done = f32[32,128,256]{2,1,0:T(8,128)S(1)} copy-done((f32[32,128,256]{2,1,0:T(8,128)S(1)}, f32[32,128,256]{2,1,0:T(8,128)}, u32[]{:S(2)}) %copy-start) | copy-done | bytes 4194328
  2.8 0.0 copy-start.1
  2.8 0.9 %copy-done.1 = f32[128,256]{1,0:T(8,128)S(1)} copy-done((f32[128,256]{1,0:T(8,128)S(1)}, f32[128,256]{1,0:T(8,128)}, u32[]{:S(2)}) %copy-start.1) | copy-done | bytes 131096
  3.7 0.0 copy-start.2
  3.7 0.8 %copy-done.2 = f32[32,256]{1,0:T(8,128)S(1)} copy-done((f32[32,256]{1,0:T(8,128)S(1)}, f32[32,256]{1,0:T(8,128)}, u32[]{:S(2)}) %copy-start.2) | copy-done | bytes 32792
  4.5 0.0 copy-start.3
  4.5 0.7 %copy-done.3 = f32[256]{0:T(256)S(1)} copy-done((f32[256]{0:T(256)S(1)}, f32[256]{0:T(256)}, u32[]{:S(2)}) %copy-start.3) | copy-done | bytes 1048
  5.2 0.0 copy-start.4
  5.2 0.7 %copy-done.4 = f32[5]{0:T(128)S(1)} copy-done((f32[5]{0:T(128)S(1)}, f32[5]{0:T(128)}, u32[]{:S(2)}) %copy-start.4) | copy-done | bytes 44
  5.8 26.4 %exchange.1 = (f32[128,256]{1,0:T(8,128)S(1)}, f32[32,256]{1,0:T(8,128)S(1)}, f32[128,256]{1,0:T(8,128)S(1)}, f32[32,256]{1,0:T(8,128)S(1)}) custom-call(f32[32,128,256]{2,1,0:T(8,128)S(1)} %copy-done, f32[128,256]{1,0:T(8,128)S(1)} %copy-done.1, f32[1,256]{1,0:T(1,128)S(1)} %bitcast.1, f32[5]{0:T(128)S(1)} %copy-done.4, f32[32,256]{1,0:T(8,128)S(1)} %copy-done.2), custom_call_target="tpu_custom_call" | custom-call | tf_op jit(solution)/shard_map/exchange/pallas_call | solution.py:332
  32.3 4.5 %descent.1 = (f32[32,128,256]{2,1,0:T(8,128)}, f32[32,32]{1,0:T(8,128)}) custom-call(f32[32,128,256]{2,1,0:T(8,128)S(1)} %copy-done, f32[128,256]{1,0:T(8,128)S(1)} %get-tuple-element.6.light_ref, f32[128,256]{1,0:T(8,128)S(1)} %get-tuple-element.7.after_ref, f32[32,256]{1,0:T(8,128)S(1)} %get-tuple-element.8.back_ref, f32[1,256]{1,0:T(1,128)S(1)} %bitcast.2, ...), custom_call_target="tpu_custom_call" | custom-call | tf_op jit(solution)/shard_map/descent/pallas_call | solution.py:408
Async XLA Ops:
  0.6 2.2 %copy-start = (f32[32,128,256]{2,1,0:T(8,128)S(1)}, f32[32,128,256]{2,1,0:T(8,128)}, u32[]{:S(2)}) copy-start(f32[32,128,256]{2,1,0:T(8,128)} %c_ref.1) | copy-start | bytes 12582916
  2.8 0.9 %copy-start.1 = (f32[128,256]{1,0:T(8,128)S(1)}, f32[128,256]{1,0:T(8,128)}, u32[]{:S(2)}) copy-start(f32[128,256]{1,0:T(8,128)} %entry.1) | copy-start | bytes 393220
  3.7 0.8 %copy-start.2 = (f32[32,256]{1,0:T(8,128)S(1)}, f32[32,256]{1,0:T(8,128)}, u32[]{:S(2)}) copy-start(f32[32,256]{1,0:T(8,128)} %measured.1) | copy-start | bytes 98308
  4.5 0.7 %copy-start.3 = (f32[256]{0:T(256)S(1)}, f32[256]{0:T(256)}, u32[]{:S(2)}) copy-start(f32[256]{0:T(256)} %param.7) | copy-start | bytes 3076
  5.2 0.7 %copy-start.4 = (f32[5]{0:T(128)S(1)}, f32[5]{0:T(128)}, u32[]{:S(2)}) copy-start(f32[5]{0:T(128)} %taps_ref.1) | copy-start | bytes 64

commit v2 on v1

v2 whole, which is shorter than its diff:
```python
import functools

import jax
import jax.numpy as jnp
from jax import lax
from jax.experimental import pallas as pl
from jax.experimental.pallas import tpu as pltpu
from jax.sharding import PartitionSpec as P

MESH = pl.DeviceIdType.MESH
ROWS, LANES = 8, 128
SUBS = 2
WRITES = 8


def blur(x, taps, sign):
    width = x.shape[1]
    lane = lax.broadcasted_iota(jnp.int32, x.shape, 1)
    total = jnp.zeros_like(x)
    for k in range(5):
        step = sign * (k - 2)
        moved = x if step == 0 else pltpu.roll(x, (-step) % width, 1)
        inside = (lane + step >= 0) & (lane + step < width)
        total = total + taps[k] * jnp.where(inside, moved, 0.0)
    return total


def exchange_kernel(
    nb, nd, c_hbm, entry_hbm, absorb_hbm, taps_hbm, measured_hbm,
    trans, later_out, res_out,
    w, entry, absorb, taps_ref, measured, light, wide, tot, pbuf, ps, qbuf, fs, fbuf, before,
    img, rs, ag,
    load_sem, small_sem, a_send, a_recv, b_send, b_recv, f_send, f_recv,
    rs_send, rs_recv, ag_send, ag_recv,
):
    cells, depth, height = w.shape
    half = depth // 2
    sub = half // SUBS
    pairs = nb // 2
    bi = lax.axis_index("beam")
    di = lax.axis_index("depth")
    core = lax.rem(bi, 2)
    pair = bi // 2
    partner = bi + 1 - 2 * core
    tiles = depth // ROWS
    lane_blocks = height // LANES
    pieces = (cells // ROWS) * lane_blocks
    owners = min(nd, pieces)
    per = pieces // owners

    own_start = pl.multiple_of(core * half, ROWS)
    other_start = pl.multiple_of((1 - core) * half, ROWS)
    own_rows = pl.ds(own_start, half)
    other_rows = pl.ds(other_start, half)

    def at(start, s):
        return pl.ds(pl.multiple_of(start + s * sub, ROWS), sub)

    loads = []
    for start in (other_start, own_start):
        for s in range(SUBS):
            part = at(start, s)
            copy = pltpu.make_async_copy(
                c_hbm.at[:, part, :], w.at[:, part, :], load_sem.at[len(loads)]
            )
            copy.start()
            loads.append(copy)
    small = []
    for source, place in (
        (absorb_hbm, absorb), (entry_hbm, entry), (taps_hbm, taps_ref), (measured_hbm, measured)
    ):
        copy = pltpu.make_async_copy(source, place, small_sem.at[len(small)])
        copy.start()
        small.append(copy)

    barrier = pltpu.get_barrier_semaphore()
    for k in range(1, nb):
        pl.semaphore_signal(
            barrier, inc=1, device_id={"beam": lax.rem(bi + k, nb)}, device_id_type=MESH
        )
    for k in range(1, nd):
        pl.semaphore_signal(
            barrier, inc=1, device_id={"depth": lax.rem(di + k, nd)}, device_id_type=MESH
        )

    def sum_cells(start, s):
        def tile(i, carry):
            rows = pl.ds(pl.multiple_of(start + s * sub + i * ROWS, ROWS), ROWS)
            parts = [w[b, rows, :] for b in range(4)]
            for b in range(4, cells):
                parts[b % 4] = parts[b % 4] + w[b, rows, :]
            tot[0, rows, :] = (parts[0] + parts[1]) + (parts[2] + parts[3])
            return carry

        lax.fori_loop(0, sub // ROWS, tile, 0)

    def sum_weighted(start, s):
        rows = [
            pl.ds(pl.multiple_of(start + s * sub + i * ROWS, ROWS), ROWS)
            for i in range(sub // ROWS)
        ]
        for j in range(lane_blocks):
            lanes = pl.ds(j * LANES, LANES)
            acc = None
            for b in range(cells):
                factor = wide[b, :, lanes]
                terms = [factor * w[b, r, lanes] for r in rows]
                acc = terms if acc is None else [x + y for x, y in zip(acc, terms)]
            for r, x in zip(rows, acc):
                tot[1, r, lanes] = light[r, lanes] * x

    def to_partner(ph, slot):
        return pltpu.make_async_remote_copy(
            src_ref=tot.at[ph, other_rows if slot == 0 else own_rows, :],
            dst_ref=pbuf.at[ph, slot],
            send_sem=a_send.at[ph, slot],
            recv_sem=a_recv.at[ph, slot],
            device_id={"beam": partner},
            device_id_type=MESH,
        )

    def to_pair(ph, target, s):
        return pltpu.make_async_remote_copy(
            src_ref=ps.at[ph, s],
            dst_ref=qbuf.at[ph, pair, s],
            send_sem=b_send.at[ph, target, s],
            recv_sem=b_recv.at[ph, pair, s],
            device_id={"beam": 2 * target + core},
            device_id_type=MESH,
        )

    def from_pair(ph, source, s):
        return pltpu.make_async_remote_copy(
            src_ref=ps.at[ph, s],
            dst_ref=qbuf.at[ph, source, s],
            send_sem=b_send.at[ph, source, s],
            recv_sem=b_recv.at[ph, source, s],
            device_id={"beam": 2 * source + core},
            device_id_type=MESH,
        )

    def forward(ph, s):
        return pltpu.make_async_remote_copy(
            src_ref=fs.at[ph, s],
            dst_ref=fbuf.at[ph, s],
            send_sem=f_send.at[ph, s],
            recv_sem=f_recv.at[ph, s],
            device_id={"beam": partner},
            device_id_type=MESH,
        )

    def downstream(ph, other):
        return other > pair if ph == 0 else other < pair

    def upstream(ph, other):
        return other < pair if ph == 0 else other > pair

    def exchange_begin(ph, sums):
        for s in range(SUBS):
            sums(other_start, s)
        if ph == 0:
            pl.semaphore_wait(barrier, nb - 1 + nd - 1)
        to_partner(ph, 0).start()
        for s in range(SUBS):
            sums(own_start, s)
            if s == 0:
                to_partner(ph, 0).wait_recv()
            if pairs > 1:
                ps[ph, s] = tot[ph, at(own_start, s), :] + pbuf[ph, 0, s * sub:(s + 1) * sub, :]
                for target in range(pairs):
                    @pl.when(downstream(ph, target))
                    def _():
                        to_pair(ph, target, s).start()
        to_partner(ph, 1).start()

    def exchange_end(ph, result):
        first = 0 if ph == 0 else pairs - 1
        if pairs > 1:
            @pl.when(upstream(ph, first))
            def _():
                for s in range(SUBS):
                    from_pair(ph, first, s).wait_recv()
                    fs[ph, s] = qbuf[ph, first, s]
                    for source in range(pairs):
                        if source != first:
                            @pl.when(upstream(ph, source))
                            def _():
                                from_pair(ph, source, s).wait_recv()
                                fs[ph, s] = fs[ph, s] + qbuf[ph, source, s]
                    forward(ph, s).start()

        to_partner(ph, 1).wait_recv()
        takes = core == (1 if ph == 0 else 0)

        @pl.when(takes)
        def _():
            result[own_rows, :] = pbuf[ph, 0]
            result[other_rows, :] = pbuf[ph, 1]

        @pl.when(jnp.logical_not(takes))
        def _():
            result[...] = jnp.zeros_like(result)

        if pairs > 1:
            @pl.when(upstream(ph, first))
            def _():
                for s in range(SUBS):
                    mine, theirs = at(own_start, s), at(other_start, s)
                    result[mine, :] = result[mine, :] + fs[ph, s]
                    forward(ph, s).wait_recv()
                    result[theirs, :] = result[theirs, :] + fbuf[ph, s]

    def exchange_sent(ph):
        to_partner(ph, 0).wait_send()
        to_partner(ph, 1).wait_send()
        if pairs > 1:
            for s in range(SUBS):
                for target in range(pairs):
                    @pl.when(downstream(ph, target))
                    def _():
                        to_pair(ph, target, s).wait_send()

                @pl.when(upstream(ph, 0 if ph == 0 else pairs - 1))
                def _():
                    forward(ph, s).wait_send()

    def sum_loaded(start, s):
        loads[s if start is other_start else SUBS + s].wait()
        sum_cells(start, s)

    exchange_begin(0, sum_loaded)
    for copy in small:
        copy.wait()

    def weigh(i, carry):
        rows = pl.ds(pl.multiple_of(i * ROWS, ROWS), ROWS)
        for j in range(lane_blocks):
            lanes = pl.ds(j * LANES, LANES)
            rate = -absorb[:, lanes]
            prior = w[0, rows, lanes]
            for b in range(1, cells):
                c = w[b, rows, lanes]
                passed = jnp.exp(rate * prior)
                trans[b, rows, lanes] = passed
                w[b, rows, lanes] = c * passed
                prior = prior + c
        return carry

    lax.fori_loop(0, tiles, weigh, 0)

    exchange_end(0, before)
    light[...] = entry[...] * jnp.exp(-absorb[...] * before[...])

    def emit(g, carry):
        for j in range(lane_blocks):
            lanes = pl.ds(j * LANES, LANES)
            sums = []
            for r in range(ROWS):
                acc = [None, None]
                for t in range(tiles):
                    rows = pl.ds(t * ROWS, ROWS)
                    term = light[rows, lanes] * w[g * ROWS + r, rows, lanes]
                    acc[t % 2] = term if acc[t % 2] is None else acc[t % 2] + term
                sums.append(jnp.sum(acc[0] + acc[1], axis=0, keepdims=True))
            img[g * lane_blocks + j] = jnp.concatenate(sums, axis=0)
        return carry

    lax.fori_loop(0, cells // ROWS, emit, 0)

    def guarded(index, body):
        if owners == nd:
            body()
        else:
            pl.when(index < owners)(body)

    def scatter(target, k):
        return pltpu.make_async_remote_copy(
            src_ref=img.at[pl.ds(target * per, per)],
            dst_ref=rs.at[di],
            send_sem=rs_send.at[k],
            recv_sem=rs_recv.at[di],
            device_id={"depth": target},
            device_id_type=MESH,
        )

    def scattered(source, k):
        return pltpu.make_async_remote_copy(
            src_ref=img.at[pl.ds(0, per)],
            dst_ref=rs.at[source],
            send_sem=rs_send.at[k],
            recv_sem=rs_recv.at[source],
            device_id={"depth": source},
            device_id_type=MESH,
        )

    def gather(target, k):
        mine = pl.ds(di * per, per)
        return pltpu.make_async_remote_copy(
            src_ref=ag.at[mine],
            dst_ref=ag.at[mine],
            send_sem=ag_send.at[k],
            recv_sem=ag_recv.at[di],
            device_id={"depth": target},
            device_id_type=MESH,
        )

    def gathered(source, k):
        theirs = pl.ds(source * per, per)
        return pltpu.make_async_remote_copy(
            src_ref=ag.at[theirs],
            dst_ref=ag.at[theirs],
            send_sem=ag_send.at[k],
            recv_sem=ag_recv.at[source],
            device_id={"depth": source},
            device_id_type=MESH,
        )

    for k in range(1, nd):
        target = lax.rem(di + k, nd)
        guarded(target, lambda target=target, k=k: scatter(target, k).start())

    def reduce_own():
        total = img[pl.ds(di * per, per)]
        for k in range(1, nd):
            source = lax.rem(di + k, nd)
            scattered(source, k).wait_recv()
            total = total + rs[source]
        ag[pl.ds(di * per, per)] = total * (1.0 / (depth * nd))
        for k in range(1, nd):
            gather(lax.rem(di + k, nd), k).start()

    guarded(di, reduce_own)

    for k in range(1, nd):
        source = lax.rem(di + k, nd)
        guarded(source, lambda source=source, k=k: gathered(source, k).wait_recv())

    image = jnp.concatenate(
        [
            jnp.concatenate([ag[g * lane_blocks + j] for j in range(lane_blocks)], axis=1)
            for g in range(cells // ROWS)
        ],
        axis=0,
    )
    taps = [taps_ref[k] for k in range(5)]
    residual = blur(image, taps, 1) - measured[...]
    res_out[...] = residual
    back = blur(residual, taps, -1)
    for b in range(cells):
        wide[b] = jnp.broadcast_to(back[b:b + 1, :], (ROWS, height))

    exchange_begin(1, sum_weighted)

    def adjoint(i, carry):
        rows = pl.ds(pl.multiple_of(i * ROWS, ROWS), ROWS)
        for j in range(lane_blocks):
            lanes = pl.ds(j * LANES, LANES)
            rate, lamp = absorb[:, lanes], light[rows, lanes]
            later = None
            for b in reversed(range(cells)):
                scale = lamp * wide[b, :, lanes]
                q = scale if b == 0 else scale * trans[b, rows, lanes]
                trans[b, rows, lanes] = -q if later is None else rate * later - q
                if b > 0:
                    term = scale * w[b, rows, lanes]
                    later = term if later is None else later + term
        return carry

    lax.fori_loop(0, tiles, adjoint, 0)
    exchange_end(1, before)
    later_out[...] = absorb[...] * before[...]

    exchange_sent(0)
    exchange_sent(1)
    for k in range(1, nd):
        target = lax.rem(di + k, nd)
        guarded(target, lambda target=target, k=k: scatter(target, k).wait_send())

    def sent():
        for k in range(1, nd):
            gather(lax.rem(di + k, nd), k).wait_send()

    guarded(di, sent)


def in_hbm(x):
    return pltpu.with_memory_space_constraint(x, pltpu.HBM)


def exchange(nb, nd, concentration, entry, absorb, taps, measured):
    cells, depth, height = concentration.shape
    half, pairs = depth // 2, nb // 2
    sub = half // SUBS
    pieces = (cells // ROWS) * (height // LANES)
    per = pieces // min(nd, pieces)
    f32 = jnp.float32
    dma = pltpu.SemaphoreType.DMA
    vmem = pl.BlockSpec(memory_space=pltpu.VMEM)
    return pl.pallas_call(
        functools.partial(exchange_kernel, nb, nd),
        out_shape=[
            jax.ShapeDtypeStruct((cells, depth, height), f32),
            jax.ShapeDtypeStruct((depth, height), f32),
            jax.ShapeDtypeStruct((cells, height), f32),
        ],
        in_specs=[pl.BlockSpec(memory_space=pltpu.HBM)] * 5,
        out_specs=[vmem] * 3,
        scratch_shapes=[
            pltpu.VMEM((cells, depth, height), f32),
            pltpu.VMEM((depth, height), f32),
            pltpu.VMEM(absorb.shape, f32),
            pltpu.SMEM(taps.shape, f32),
            pltpu.VMEM((cells, height), f32),
            pltpu.VMEM((depth, height), f32),
            pltpu.VMEM((cells, ROWS, height), f32),
            pltpu.VMEM((2, depth, height), f32),
            pltpu.VMEM((2, 2, half, height), f32),
            pltpu.VMEM((2, SUBS, sub, height), f32),
            pltpu.VMEM((2, pairs, SUBS, sub, height), f32),
            pltpu.VMEM((2, SUBS, sub, height), f32),
            pltpu.VMEM((2, SUBS, sub, height), f32),
            pltpu.VMEM((depth, height), f32),
            pltpu.VMEM((pieces, ROWS, LANES), f32),
            pltpu.VMEM((nd, per, ROWS, LANES), f32),
            pltpu.VMEM((pieces, ROWS, LANES), f32),
            dma((2 * SUBS,)), dma((4,)), dma((2, 2)), dma((2, 2)),
            dma((2, pairs, SUBS)), dma((2, pairs, SUBS)), dma((2, SUBS)), dma((2, SUBS)),
            dma((nd,)), dma((nd,)), dma((nd,)), dma((nd,)),
        ],
        compiler_params=pltpu.CompilerParams(
            collective_id=0, has_side_effects=True, vmem_limit_bytes=24 * 2**20
        ),
        name="exchange",
    )(*(in_hbm(x) for x in (concentration, entry, absorb, taps, measured)))


def descent_kernel(nd, part_ref, later_ref, res_ref, out_hbm, res_hbm, stage, res_stage, sems, res_sem):
    cells, depth, height = part_ref.shape
    width = height // nd
    di = lax.axis_index("depth")
    group = cells // WRITES

    for n in range(WRITES):
        def tile(i, carry):
            rows = pl.ds(pl.multiple_of(i * ROWS, ROWS), ROWS)
            later = later_ref[rows, :]
            for b in range(n * group, (n + 1) * group):
                stage[b, rows, :] = part_ref[b, rows, :] + later
            return carry

        lax.fori_loop(0, depth // ROWS, tile, 0)
        part = pl.ds(n * group, group)
        pltpu.make_async_copy(stage.at[part], out_hbm.at[part], sems.at[n]).start()

    for k in range(nd):
        @pl.when(di == k)
        def _():
            res_stage[...] = res_ref[:, k * width:(k + 1) * width]
    residual = pltpu.make_async_copy(res_stage, res_hbm, res_sem.at[0])
    residual.start()
    for n in range(WRITES):
        part = pl.ds(n * group, group)
        pltpu.make_async_copy(stage.at[part], out_hbm.at[part], sems.at[n]).wait()
    residual.wait()


def write_descent(nd, part, later, residual):
    cells, depth, height = part.shape
    f32 = jnp.float32
    shapes = (part.shape, (cells, height // nd))
    return pl.pallas_call(
        functools.partial(descent_kernel, nd),
        out_shape=[jax.ShapeDtypeStruct(shape, f32) for shape in shapes],
        in_specs=[pl.BlockSpec(memory_space=pltpu.VMEM)] * 3,
        out_specs=[pl.BlockSpec(memory_space=pltpu.HBM)] * 2,
        scratch_shapes=[
            pltpu.VMEM(shapes[0], f32),
            pltpu.VMEM(shapes[1], f32),
            pltpu.SemaphoreType.DMA((WRITES,)),
            pltpu.SemaphoreType.DMA((1,)),
        ],
        compiler_params=pltpu.CompilerParams(vmem_limit_bytes=24 * 2**20),
        name="descent",
    )(part, later, residual)


def solution(mesh):
    nb, nd = mesh.shape["beam"], mesh.shape["depth"]

    def local(concentration, entry_intensity, absorb, blur_taps, measured):
        part, later, residual = exchange(
            nb, nd, concentration, entry_intensity, absorb.reshape(1, -1), blur_taps, measured
        )
        return tuple(write_descent(nd, part, later, residual))

    return jax.shard_map(
        local,
        mesh=mesh,
        in_specs=(P("beam", "depth", None), P("depth", None), P(), P(), P("beam", None)),
        out_specs=(P("beam", "depth", None), P("beam", "depth")),
        check_vma=False,
    )
```

time: 37 us -> 28.1 us (0.76)
  local copies, waits for them, and re-layouts: 5.18 us -> 0 us
  Pallas kernels: 30.9 us -> 27.3 us
    unnamed x10 -> x0, local copies, waits for them, and re-layouts: 5.18 us -> none
    pallas_call x1, Pallas kernels: 4.5 us -> 2.2 us  [write_descent(): pl.pallas_call(functools.partial(descent_kernel, nd), out_shape=[jax.Shap...]
    pallas_call x1, Pallas kernels: 26.4 us -> 25.1 us  [exchange(): pl.pallas_call(functools.partial(exchange_kernel, nb, nd), out_shape=[jax...]
where the time goes in v2:
time: 28.1 us; the launch traced here: 27.9 us
  Pallas kernels  27.3 us (97%)
  between operations  0.64 us (2%)
    pallas_call x1, Pallas kernels, exchange(): pl.pallas_call(functools.partial(exchange_kernel, nb, nd), out_shape=[jax...  25.1 us
    pallas_call x1, Pallas kernels, write_descent(): pl.pallas_call(functools.partial(descent_kernel, nd), out_shape=[jax.Shap...  2.2 us

profile of v2, /device:TPU:0, one launch (start us, length us, event | category | flops | bytes accessed | tf_op | source)
XLA Modules:
  0.0 27.9 jit_solution(6869671762544829370)
XLA Ops:
  0.6 25.1 %exchange.1 = (f32[32,128,256]{2,1,0:T(8,128)S(1)}, f32[128,256]{1,0:T(8,128)S(1)}, f32[32,256]{1,0:T(8,128)S(1)}) custom-call(f32[32,128,256]{2,1,0:T(8,128)} %c_hbm.1, f32[128,256]{1,0:T(8,128)} %entry_hbm.1, f32[1,256]{1,0:T(1,128)} %bitcast.1, f32[5]{0:T(128)} %taps_hbm.1, f32[32,256]{1,0:T(8,128)} %measured_hbm.1), custom_call_target="tpu_custom_call" | custom-call | tf_op jit(solution)/shard_map/exchange/pallas_call | solution.py:399
  25.8 2.2 %descent.1 = (f32[32,128,256]{2,1,0:T(8,128)}, f32[32,32]{1,0:T(8,128)}) custom-call(f32[32,128,256]{2,1,0:T(8,128)S(1)} %get-tuple-element.5.part_ref, f32[128,256]{1,0:T(8,128)S(1)} %get-tuple-element.6.later_ref, f32[32,256]{1,0:T(8,128)S(1)} %get-tuple-element.7.res_ref), custom_call_target="tpu_custom_call" | custom-call | tf_op jit(solution)/shard_map/descent/pallas_call | solution.py:471

commit v3 on v2

--- a/solution.py
+++ b/solution.py
@@ -9,7 +9,8 @@
 
 MESH = pl.DeviceIdType.MESH
 ROWS, LANES = 8, 128
-SUBS = 2
+SUBS = 4
+DIRECT = 2
 WRITES = 8
 
 
@@ -28,14 +29,15 @@
 def exchange_kernel(
     nb, nd, c_hbm, entry_hbm, absorb_hbm, taps_hbm, measured_hbm,
     trans, later_out, res_out,
-    w, entry, absorb, taps_ref, measured, light, wide, tot, pbuf, ps, qbuf, fs, fbuf, before,
+    w, entry, absorb, taps_ref, measured, light, wide, tot, pbuf, ps, qbuf, dbuf, fs, fbuf, before,
     img, rs, ag,
-    load_sem, small_sem, a_send, a_recv, b_send, b_recv, f_send, f_recv,
+    load_sem, small_sem, a_send, a_recv, b_send, b_recv, d_send, d_recv, f_send, f_recv,
     rs_send, rs_recv, ag_send, ag_recv,
 ):
     cells, depth, height = w.shape
     half = depth // 2
     sub = half // SUBS
+    relayed = SUBS - DIRECT
     pairs = nb // 2
     bi = lax.axis_index("beam")
     di = lax.axis_index("depth")
@@ -139,6 +141,26 @@
             device_id_type=MESH,
         )
 
+    def to_cross(ph, target, s):
+        return pltpu.make_async_remote_copy(
+            src_ref=ps.at[ph, s],
+            dst_ref=dbuf.at[ph, pair, s - relayed],
+            send_sem=d_send.at[ph, target, s - relayed],
+            recv_sem=d_recv.at[ph, pair, s - relayed],
+            device_id={"beam": 2 * target + 1 - core},
+            device_id_type=MESH,
+        )
+
+    def from_cross(ph, source, s):
+        return pltpu.make_async_remote_copy(
+            src_ref=ps.at[ph, s],
+            dst_ref=dbuf.at[ph, source, s - relayed],
+            send_sem=d_send.at[ph, source, s - relayed],
+            recv_sem=d_recv.at[ph, source, s - relayed],
+            device_id={"beam": 2 * source + 1 - core},
+            device_id_type=MESH,
+        )
+
     def forward(ph, s):
         return pltpu.make_async_remote_copy(
             src_ref=fs.at[ph, s],
@@ -171,44 +193,75 @@
                     @pl.when(downstream(ph, target))
                     def _():
                         to_pair(ph, target, s).start()
+                        if s >= relayed:
+                            to_cross(ph, target, s).start()
         to_partner(ph, 1).start()
 
-    def exchange_end(ph, result):
+    def collect(ph, s):
         first = 0 if ph == 0 else pairs - 1
+        from_pair(ph, first, s).wait_recv()
+        fs[ph, s] = qbuf[ph, first, s]
+        for source in range(pairs):
+            if source != first:
+                @pl.when(upstream(ph, source))
+                def _():
+                    from_pair(ph, source, s).wait_recv()
+                    fs[ph, s] = fs[ph, s] + qbuf[ph, source, s]
+
+    def when_upstream(ph, body):
         if pairs > 1:
-            @pl.when(upstream(ph, first))
-            def _():
-                for s in range(SUBS):
-                    from_pair(ph, first, s).wait_recv()
-                    fs[ph, s] = qbuf[ph, first, s]
-                    for source in range(pairs):
-                        if source != first:
-                            @pl.when(upstream(ph, source))
-                            def _():
-                                from_pair(ph, source, s).wait_recv()
-                                fs[ph, s] = fs[ph, s] + qbuf[ph, source, s]
-                    forward(ph, s).start()
-
-        to_partner(ph, 1).wait_recv()
+            pl.when(upstream(ph, 0 if ph == 0 else pairs - 1))(body)
+
+    def relay(ph):
+        def body():
+            for s in range(relayed):
+                collect(ph, s)
+                forward(ph, s).start()
+
+        when_upstream(ph, body)
+
+    def from_core(ph, slot, result):
         takes = core == (1 if ph == 0 else 0)
+        rows = own_rows if slot == 0 else other_rows
 
         @pl.when(takes)
         def _():
-            result[own_rows, :] = pbuf[ph, 0]
-            result[other_rows, :] = pbuf[ph, 1]
+            result[rows, :] = pbuf[ph, slot]
 
         @pl.when(jnp.logical_not(takes))
         def _():
-            result[...] = jnp.zeros_like(result)
-
-        if pairs > 1:
-            @pl.when(upstream(ph, first))
-            def _():
-                for s in range(SUBS):
-                    mine, theirs = at(own_start, s), at(other_start, s)
-                    result[mine, :] = result[mine, :] + fs[ph, s]
+            result[rows, :] = jnp.zeros((half, height), jnp.float32)
+
+    def finish_own(ph, result):
+        from_core(ph, 0, result)
+
+        def body():
+            for s in range(SUBS):
+                if s >= relayed:
+                    collect(ph, s)
+                rows = at(own_start, s)
+                result[rows, :] = result[rows, :] + fs[ph, s]
+
+        when_upstream(ph, body)
+
+    def finish_other(ph, result):
+        to_partner(ph, 1).wait_recv()
+        from_core(ph, 1, result)
+
+        def body():
+            for s in range(SUBS):
+                rows = at(other_start, s)
+                if s < relayed:
                     forward(ph, s).wait_recv()
-                    result[theirs, :] = result[theirs, :] + fbuf[ph, s]
+                    result[rows, :] = result[rows, :] + fbuf[ph, s]
+                else:
+                    for source in range(pairs):
+                        @pl.when(upstream(ph, source))
+                        def _():
+                            from_cross(ph, source, s).wait_recv()
+                            result[rows, :] = result[rows, :] + dbuf[ph, source, s - relayed]
+
+        when_upstream(ph, body)
 
     def exchange_sent(ph):
         to_partner(ph, 0).wait_send()
@@ -219,9 +272,12 @@
                     @pl.when(downstream(ph, target))
                     def _():
                         to_pair(ph, target, s).wait_send()
-
-                @pl.when(upstream(ph, 0 if ph == 0 else pairs - 1))
-                def _():
+                        if s >= relayed:
+                            to_cross(ph, target, s).wait_send()
+
+            @pl.when(upstream(ph, 0 if ph == 0 else pairs - 1))
+            def _():
+                for s in range(relayed):
                     forward(ph, s).wait_send()
 
     def sum_loaded(start, s):
@@ -232,40 +288,64 @@
     for copy in small:
         copy.wait()
 
-    def weigh(i, carry):
-        rows = pl.ds(pl.multiple_of(i * ROWS, ROWS), ROWS)
-        for j in range(lane_blocks):
-            lanes = pl.ds(j * LANES, LANES)
-            rate = -absorb[:, lanes]
-            prior = w[0, rows, lanes]
-            for b in range(1, cells):
-                c = w[b, rows, lanes]
-                passed = jnp.exp(rate * prior)
-                trans[b, rows, lanes] = passed
-                w[b, rows, lanes] = c * passed
-                prior = prior + c
-        return carry
-
-    lax.fori_loop(0, tiles, weigh, 0)
-
-    exchange_end(0, before)
-    light[...] = entry[...] * jnp.exp(-absorb[...] * before[...])
-
-    def emit(g, carry):
-        for j in range(lane_blocks):
-            lanes = pl.ds(j * LANES, LANES)
-            sums = []
-            for r in range(ROWS):
-                acc = [None, None]
-                for t in range(tiles):
-                    rows = pl.ds(t * ROWS, ROWS)
-                    term = light[rows, lanes] * w[g * ROWS + r, rows, lanes]
-                    acc[t % 2] = term if acc[t % 2] is None else acc[t % 2] + term
-                sums.append(jnp.sum(acc[0] + acc[1], axis=0, keepdims=True))
-            img[g * lane_blocks + j] = jnp.concatenate(sums, axis=0)
-        return carry
-
-    lax.fori_loop(0, cells // ROWS, emit, 0)
+    def weigh(start, first, last):
+        def tile(i, carry):
+            rows = pl.ds(pl.multiple_of(start + i * ROWS, ROWS), ROWS)
+            for j in range(lane_blocks):
+                lanes = pl.ds(j * LANES, LANES)
+                rate = -absorb[:, lanes]
+                prior = w[0, rows, lanes]
+                for b in range(1, cells):
+                    c = w[b, rows, lanes]
+                    passed = jnp.exp(rate * prior)
+                    trans[b, rows, lanes] = passed
+                    w[b, rows, lanes] = c * passed
+                    prior = prior + c
+            return carry
+
+        lax.fori_loop(first, last, tile, 0)
+
+    def enter(rows):
+        light[rows, :] = entry[rows, :] * jnp.exp(-absorb[...] * before[rows, :])
+
+    def emit(start, last):
+        def group(g, carry):
+            for j in range(lane_blocks):
+                lanes = pl.ds(j * LANES, LANES)
+                tile_rows = [
+                    pl.ds(pl.multiple_of(start + t * ROWS, ROWS), ROWS)
+                    for t in range(half // ROWS)
+                ]
+                lamps = [light[rows, lanes] for rows in tile_rows]
+                sums = []
+                for r in range(ROWS):
+                    b = g * ROWS + r
+                    acc = [wide[b, :, lanes] if last else None, None]
+                    for t, rows in enumerate(tile_rows):
+                        term = lamps[t] * w[b, rows, lanes]
+                        acc[t % 2] = term if acc[t % 2] is None else acc[t % 2] + term
+                    total = acc[0] + acc[1]
+                    if last:
+                        sums.append(jnp.sum(total, axis=0, keepdims=True))
+                    else:
+                        wide[b, :, lanes] = total
+                if last:
+                    img[g * lane_blocks + j] = jnp.concatenate(sums, axis=0)
+            return carry
+
+        lax.fori_loop(0, cells // ROWS, group, 0)
+
+    half_tiles = half // ROWS
+    weigh(own_start, 0, half_tiles)
+    weigh(other_start, 0, half_tiles // 2)
+    relay(0)
+    weigh(other_start, half_tiles // 2, half_tiles)
+    finish_own(0, before)
+    enter(own_rows)
+    emit(own_start, False)
+    finish_other(0, before)
+    enter(other_rows)
+    emit(other_start, True)
 
     def guarded(index, body):
         if owners == nd:
@@ -367,7 +447,9 @@
         return carry
 
     lax.fori_loop(0, tiles, adjoint, 0)
-    exchange_end(1, before)
+    relay(1)
+    finish_own(1, before)
+    finish_other(1, before)
     later_out[...] = absorb[...] * before[...]
 
     exchange_sent(0)
@@ -417,6 +499,7 @@
             pltpu.VMEM((2, 2, half, height), f32),
             pltpu.VMEM((2, SUBS, sub, height), f32),
             pltpu.VMEM((2, pairs, SUBS, sub, height), f32),
+            pltpu.VMEM((2, pairs, DIRECT, sub, height), f32),
             pltpu.VMEM((2, SUBS, sub, height), f32),
             pltpu.VMEM((2, SUBS, sub, height), f32),
             pltpu.VMEM((depth, height), f32),
@@ -424,7 +507,8 @@
             pltpu.VMEM((nd, per, ROWS, LANES), f32),
             pltpu.VMEM((pieces, ROWS, LANES), f32),
             dma((2 * SUBS,)), dma((4,)), dma((2, 2)), dma((2, 2)),
-            dma((2, pairs, SUBS)), dma((2, pairs, SUBS)), dma((2, SUBS)), dma((2, SUBS)),
+            dma((2, pairs, SUBS)), dma((2, pairs, SUBS)),
+            dma((2, pairs, DIRECT)), dma((2, pairs, DIRECT)), dma((2, SUBS)), dma((2, SUBS)),
             dma((nd,)), dma((nd,)), dma((nd,)), dma((nd,)),
         ],
         compiler_params=pltpu.CompilerParams(

time: 28.1 us -> 28.7 us (1.021)
  Pallas kernels: 27.3 us -> 27.9 us
    pallas_call x1, Pallas kernels: 25.1 us -> 25.7 us  [exchange(): pl.pallas_call(functools.partial(exchange_kernel, nb, nd), out_shape=[jax...]
where the time goes in v3:
time: 28.7 us; the launch traced here: 28.6 us
  Pallas kernels  27.9 us (97%)
  between operations  0.64 us (2%)
    pallas_call x1, Pallas kernels, exchange(): pl.pallas_call(functools.partial(exchange_kernel, nb, nd), out_shape=[jax...  25.7 us
    pallas_call x1, Pallas kernels, write_descent(): pl.pallas_call(functools.partial(descent_kernel, nd), out_shape=[jax.Shap...  2.2 us

profile of v3, /device:TPU:0, one launch (start us, length us, event | category | flops | bytes accessed | tf_op | source)
XLA Modules:
  0.0 28.6 jit_solution(13570349572352346905)
XLA Ops:
  0.6 25.7 %exchange.1 = (f32[32,128,256]{2,1,0:T(8,128)S(1)}, f32[128,256]{1,0:T(8,128)S(1)}, f32[32,256]{1,0:T(8,128)S(1)}) custom-call(f32[32,128,256]{2,1,0:T(8,128)} %c_hbm.1, f32[128,256]{1,0:T(8,128)} %entry_hbm.1, f32[1,256]{1,0:T(1,128)} %bitcast.1, f32[5]{0:T(128)} %taps_hbm.1, f32[32,256]{1,0:T(8,128)} %measured_hbm.1), custom_call_target="tpu_custom_call" | custom-call | tf_op jit(solution)/shard_map/exchange/pallas_call | solution.py:481
  26.4 2.2 %descent.1 = (f32[32,128,256]{2,1,0:T(8,128)}, f32[32,32]{1,0:T(8,128)}) custom-call(f32[32,128,256]{2,1,0:T(8,128)S(1)} %get-tuple-element.5.part_ref, f32[128,256]{1,0:T(8,128)S(1)} %get-tuple-element.6.later_ref, f32[32,256]{1,0:T(8,128)S(1)} %get-tuple-element.7.res_ref), custom_call_target="tpu_custom_call" | custom-call | tf_op jit(solution)/shard_map/descent/pallas_call | solution.py:555

commit v4 on v2

--- a/solution.py
+++ b/solution.py
@@ -9,7 +9,8 @@
 
 MESH = pl.DeviceIdType.MESH
 ROWS, LANES = 8, 128
-SUBS = 2
+SUBS = (2, 4)
+DIRECT = (0, 2)
 WRITES = 8
 
 
@@ -27,15 +28,16 @@
 
 def exchange_kernel(
     nb, nd, c_hbm, entry_hbm, absorb_hbm, taps_hbm, measured_hbm,
-    trans, later_out, res_out,
-    w, entry, absorb, taps_ref, measured, light, wide, tot, pbuf, ps, qbuf, fs, fbuf, before,
+    part, later_out, res_out,
+    w, entry, absorb, taps_ref, measured, light, wide, tot, pbuf, ps, qbuf, dbuf, fs, fbuf, before,
     img, rs, ag,
-    load_sem, small_sem, a_send, a_recv, b_send, b_recv, f_send, f_recv,
+    load_sem, small_sem, a_send, a_recv, b_send, b_recv, d_send, d_recv, f_send, f_recv,
     rs_send, rs_recv, ag_send, ag_recv,
 ):
     cells, depth, height = w.shape
     half = depth // 2
-    sub = half // SUBS
+    subs = [half // n for n in SUBS]
+    relayed = [n - d for n, d in zip(SUBS, DIRECT)]
     pairs = nb // 2
     bi = lax.axis_index("beam")
     di = lax.axis_index("depth")
@@ -53,15 +55,18 @@
     own_rows = pl.ds(own_start, half)
     other_rows = pl.ds(other_start, half)
 
-    def at(start, s):
-        return pl.ds(pl.multiple_of(start + s * sub, ROWS), sub)
+    def at(ph, start, s):
+        return pl.ds(pl.multiple_of(start + s * subs[ph], ROWS), subs[ph])
+
+    def piece(ph, s):
+        return pl.ds(s * subs[ph], subs[ph])
 
     loads = []
     for start in (other_start, own_start):
-        for s in range(SUBS):
-            part = at(start, s)
+        for s in range(SUBS[0]):
+            chunk = at(0, start, s)
             copy = pltpu.make_async_copy(
-                c_hbm.at[:, part, :], w.at[:, part, :], load_sem.at[len(loads)]
+                c_hbm.at[:, chunk, :], w.at[:, chunk, :], load_sem.at[len(loads)]
             )
             copy.start()
             loads.append(copy)
@@ -85,26 +90,26 @@
 
     def sum_cells(start, s):
         def tile(i, carry):
-            rows = pl.ds(pl.multiple_of(start + s * sub + i * ROWS, ROWS), ROWS)
+            rows = pl.ds(pl.multiple_of(start + s * subs[0] + i * ROWS, ROWS), ROWS)
             parts = [w[b, rows, :] for b in range(4)]
             for b in range(4, cells):
                 parts[b % 4] = parts[b % 4] + w[b, rows, :]
             tot[0, rows, :] = (parts[0] + parts[1]) + (parts[2] + parts[3])
             return carry
 
-        lax.fori_loop(0, sub // ROWS, tile, 0)
+        lax.fori_loop(0, subs[0] // ROWS, tile, 0)
 
     def sum_weighted(start, s):
         rows = [
-            pl.ds(pl.multiple_of(start + s * sub + i * ROWS, ROWS), ROWS)
-            for i in range(sub // ROWS)
+            pl.ds(pl.multiple_of(start + s * subs[1] + i * ROWS, ROWS), ROWS)
+            for i in range(subs[1] // ROWS)
         ]
         for j in range(lane_blocks):
             lanes = pl.ds(j * LANES, LANES)
             acc = None
             for b in range(cells):
                 factor = wide[b, :, lanes]
-                terms = [factor * w[b, r, lanes] for r in rows]
+                terms = [factor * part[b, r, lanes] for r in rows]
                 acc = terms if acc is None else [x + y for x, y in zip(acc, terms)]
             for r, x in zip(rows, acc):
                 tot[1, r, lanes] = light[r, lanes] * x
@@ -121,8 +126,8 @@
 
     def to_pair(ph, target, s):
         return pltpu.make_async_remote_copy(
-            src_ref=ps.at[ph, s],
-            dst_ref=qbuf.at[ph, pair, s],
+            src_ref=ps.at[ph, piece(ph, s)],
+            dst_ref=qbuf.at[ph, pair, piece(ph, s)],
             send_sem=b_send.at[ph, target, s],
             recv_sem=b_recv.at[ph, pair, s],
             device_id={"beam": 2 * target + core},
@@ -131,18 +136,38 @@
 
     def from_pair(ph, source, s):
         return pltpu.make_async_remote_copy(
-            src_ref=ps.at[ph, s],
-            dst_ref=qbuf.at[ph, source, s],
+            src_ref=ps.at[ph, piece(ph, s)],
+            dst_ref=qbuf.at[ph, source, piece(ph, s)],
             send_sem=b_send.at[ph, source, s],
             recv_sem=b_recv.at[ph, source, s],
             device_id={"beam": 2 * source + core},
             device_id_type=MESH,
         )
 
+    def to_cross(ph, target, s):
+        return pltpu.make_async_remote_copy(
+            src_ref=ps.at[ph, piece(ph, s)],
+            dst_ref=dbuf.at[ph, pair, piece(ph, s)],
+            send_sem=d_send.at[ph, target, s],
+            recv_sem=d_recv.at[ph, pair, s],
+            device_id={"beam": 2 * target + 1 - core},
+            device_id_type=MESH,
+        )
+
+    def from_cross(ph, source, s):
+        return pltpu.make_async_remote_copy(
+            src_ref=ps.at[ph, piece(ph, s)],
+            dst_ref=dbuf.at[ph, source, piece(ph, s)],
+            send_sem=d_send.at[ph, source, s],
+            recv_sem=d_recv.at[ph, source, s],
+            device_id={"beam": 2 * source + 1 - core},
+            device_id_type=MESH,
+        )
+
     def forward(ph, s):
         return pltpu.make_async_remote_copy(
-            src_ref=fs.at[ph, s],
-            dst_ref=fbuf.at[ph, s],
+            src_ref=fs.at[ph, piece(ph, s)],
+            dst_ref=fbuf.at[ph, piece(ph, s)],
             send_sem=f_send.at[ph, s],
             recv_sem=f_recv.at[ph, s],
             device_id={"beam": partner},
@@ -156,76 +181,110 @@
         return other < pair if ph == 0 else other > pair
 
     def exchange_begin(ph, sums):
-        for s in range(SUBS):
+        for s in range(SUBS[ph]):
             sums(other_start, s)
         if ph == 0:
             pl.semaphore_wait(barrier, nb - 1 + nd - 1)
         to_partner(ph, 0).start()
-        for s in range(SUBS):
+        for s in range(SUBS[ph]):
             sums(own_start, s)
             if s == 0:
                 to_partner(ph, 0).wait_recv()
             if pairs > 1:
-                ps[ph, s] = tot[ph, at(own_start, s), :] + pbuf[ph, 0, s * sub:(s + 1) * sub, :]
+                ps[ph, piece(ph, s)] = tot[ph, at(ph, own_start, s), :] + pbuf[ph, 0, piece(ph, s)]
                 for target in range(pairs):
                     @pl.when(downstream(ph, target))
                     def _():
                         to_pair(ph, target, s).start()
+                        if s >= relayed[ph]:
+                            to_cross(ph, target, s).start()
         to_partner(ph, 1).start()
 
-    def exchange_end(ph, result):
+    def collect(ph, s):
         first = 0 if ph == 0 else pairs - 1
+        from_pair(ph, first, s).wait_recv()
+        fs[ph, piece(ph, s)] = qbuf[ph, first, piece(ph, s)]
+        for source in range(pairs):
+            if source != first:
+                @pl.when(upstream(ph, source))
+                def _():
+                    from_pair(ph, source, s).wait_recv()
+                    fs[ph, piece(ph, s)] = fs[ph, piece(ph, s)] + qbuf[ph, source, piece(ph, s)]
+
+    def when_upstream(ph, body):
         if pairs > 1:
-            @pl.when(upstream(ph, first))
-            def _():
-                for s in range(SUBS):
-                    from_pair(ph, first, s).wait_recv()
-                    fs[ph, s] = qbuf[ph, first, s]
-                    for source in range(pairs):
-                        if source != first:
-                            @pl.when(upstream(ph, source))
-                            def _():
-                                from_pair(ph, source, s).wait_recv()
-                                fs[ph, s] = fs[ph, s] + qbuf[ph, source, s]
-                    forward(ph, s).start()
-
-        to_partner(ph, 1).wait_recv()
+            pl.when(upstream(ph, 0 if ph == 0 else pairs - 1))(body)
+
+    def relay(ph):
+        def body():
+            for s in range(relayed[ph]):
+                collect(ph, s)
+                forward(ph, s).start()
+
+        when_upstream(ph, body)
+
+    def from_core(ph, slot, result):
         takes = core == (1 if ph == 0 else 0)
+        rows = own_rows if slot == 0 else other_rows
 
         @pl.when(takes)
         def _():
-            result[own_rows, :] = pbuf[ph, 0]
-            result[other_rows, :] = pbuf[ph, 1]
+            result[rows, :] = pbuf[ph, slot]
 
         @pl.when(jnp.logical_not(takes))
         def _():
-            result[...] = jnp.zeros_like(result)
-
-        if pairs > 1:
-            @pl.when(upstream(ph, first))
-            def _():
-                for s in range(SUBS):
-                    mine, theirs = at(own_start, s), at(other_start, s)
-                    result[mine, :] = result[mine, :] + fs[ph, s]
+            result[rows, :] = jnp.zeros((half, height), jnp.float32)
+
+    def finish_own(ph, result):
+        from_core(ph, 0, result)
+
+        def body():
+            for s in range(SUBS[ph]):
+                if s >= relayed[ph]:
+                    collect(ph, s)
+                rows = at(ph, own_start, s)
+                result[rows, :] = result[rows, :] + fs[ph, piece(ph, s)]
+
+        when_upstream(ph, body)
+
+    def finish_other(ph, result):
+        to_partner(ph, 1).wait_recv()
+        from_core(ph, 1, result)
+
+        def body():
+            for s in range(SUBS[ph]):
+                rows = at(ph, other_start, s)
+                if s < relayed[ph]:
                     forward(ph, s).wait_recv()
-                    result[theirs, :] = result[theirs, :] + fbuf[ph, s]
+                    result[rows, :] = result[rows, :] + fbuf[ph, piece(ph, s)]
+                else:
+                    for source in range(pairs):
+                        @pl.when(upstream(ph, source))
+                        def _():
+                            from_cross(ph, source, s).wait_recv()
+                            result[rows, :] = result[rows, :] + dbuf[ph, source, piece(ph, s)]
+
+        when_upstream(ph, body)
 
     def exchange_sent(ph):
         to_partner(ph, 0).wait_send()
         to_partner(ph, 1).wait_send()
         if pairs > 1:
-            for s in range(SUBS):
+            for s in range(SUBS[ph]):
                 for target in range(pairs):
                     @pl.when(downstream(ph, target))
                     def _():
                         to_pair(ph, target, s).wait_send()
-
-                @pl.when(upstream(ph, 0 if ph == 0 else pairs - 1))
-                def _():
+                        if s >= relayed[ph]:
+                            to_cross(ph, target, s).wait_send()
+
+            @pl.when(upstream(ph, 0 if ph == 0 else pairs - 1))
+            def _():
+                for s in range(relayed[ph]):
                     forward(ph, s).wait_send()
 
     def sum_loaded(start, s):
-        loads[s if start is other_start else SUBS + s].wait()
+        loads[s if start is other_start else SUBS[0] + s].wait()
         sum_cells(start, s)
 
     exchange_begin(0, sum_loaded)
@@ -238,18 +297,12 @@
             lanes = pl.ds(j * LANES, LANES)
             rate = -absorb[:, lanes]
             prior = w[0, rows, lanes]
+            part[0, rows, lanes] = prior
             for b in range(1, cells):
                 c = w[b, rows, lanes]
-                passed = jnp.exp(rate * prior)
-                trans[b, rows, lanes] = passed
-                w[b, rows, lanes] = c * passed
+                part[b, rows, lanes] = c * jnp.exp(rate * prior)
                 prior = prior + c
         return carry
-
-    lax.fori_loop(0, tiles, weigh, 0)
-
-    exchange_end(0, before)
-    light[...] = entry[...] * jnp.exp(-absorb[...] * before[...])
 
     def emit(g, carry):
         for j in range(lane_blocks):
@@ -259,12 +312,17 @@
                 acc = [None, None]
                 for t in range(tiles):
                     rows = pl.ds(t * ROWS, ROWS)
-                    term = light[rows, lanes] * w[g * ROWS + r, rows, lanes]
+                    term = light[rows, lanes] * part[g * ROWS + r, rows, lanes]
                     acc[t % 2] = term if acc[t % 2] is None else acc[t % 2] + term
                 sums.append(jnp.sum(acc[0] + acc[1], axis=0, keepdims=True))
             img[g * lane_blocks + j] = jnp.concatenate(sums, axis=0)
         return carry
 
+    lax.fori_loop(0, tiles, weigh, 0)
+    relay(0)
+    finish_own(0, before)
+    finish_other(0, before)
+    light[...] = entry[...] * jnp.exp(-absorb[...] * before[...])
     lax.fori_loop(0, cells // ROWS, emit, 0)
 
     def guarded(index, body):
@@ -356,18 +414,24 @@
         for j in range(lane_blocks):
             lanes = pl.ds(j * LANES, LANES)
             rate, lamp = absorb[:, lanes], light[rows, lanes]
+            prior = None
+            q = []
+            for b in range(cells):
+                scale = lamp * wide[b, :, lanes]
+                c = w[b, rows, lanes]
+                q.append(scale if b == 0 else scale * jnp.exp(-rate * prior))
+                prior = c if b == 0 else prior + c
             later = None
             for b in reversed(range(cells)):
-                scale = lamp * wide[b, :, lanes]
-                q = scale if b == 0 else scale * trans[b, rows, lanes]
-                trans[b, rows, lanes] = -q if later is None else rate * later - q
-                if b > 0:
-                    term = scale * w[b, rows, lanes]
-                    later = term if later is None else later + term
+                part[b, rows, lanes] = -q[b] if later is None else rate * later - q[b]
+                term = q[b] * w[b, rows, lanes]
+                later = term if later is None else later + term
         return carry
 
     lax.fori_loop(0, tiles, adjoint, 0)
-    exchange_end(1, before)
+    relay(1)
+    finish_own(1, before)
+    finish_other(1, before)
     later_out[...] = absorb[...] * before[...]
 
     exchange_sent(0)
@@ -390,7 +454,7 @@
 def exchange(nb, nd, concentration, entry, absorb, taps, measured):
     cells, depth, height = concentration.shape
     half, pairs = depth // 2, nb // 2
-    sub = half // SUBS
+    most = max(SUBS)
     pieces = (cells // ROWS) * (height // LANES)
     per = pieces // min(nd, pieces)
     f32 = jnp.float32
@@ -415,16 +479,18 @@
             pltpu.VMEM((cells, ROWS, height), f32),
             pltpu.VMEM((2, depth, height), f32),
             pltpu.VMEM((2, 2, half, height), f32),
-            pltpu.VMEM((2, SUBS, sub, height), f32),
-            pltpu.VMEM((2, pairs, SUBS, sub, height), f32),
-            pltpu.VMEM((2, SUBS, sub, height), f32),
-            pltpu.VMEM((2, SUBS, sub, height), f32),
+            pltpu.VMEM((2, half, height), f32),
+            pltpu.VMEM((2, pairs, half, height), f32),
+            pltpu.VMEM((2, pairs, half, height), f32),
+            pltpu.VMEM((2, half, height), f32),
+            pltpu.VMEM((2, half, height), f32),
             pltpu.VMEM((depth, height), f32),
             pltpu.VMEM((pieces, ROWS, LANES), f32),
             pltpu.VMEM((nd, per, ROWS, LANES), f32),
             pltpu.VMEM((pieces, ROWS, LANES), f32),
-            dma((2 * SUBS,)), dma((4,)), dma((2, 2)), dma((2, 2)),
-            dma((2, pairs, SUBS)), dma((2, pairs, SUBS)), dma((2, SUBS)), dma((2, SUBS)),
+            dma((2 * SUBS[0],)), dma((4,)), dma((2, 2)), dma((2, 2)),
+            dma((2, pairs, most)), dma((2, pairs, most)),
+            dma((2, pairs, most)), dma((2, pairs, most)), dma((2, most)), dma((2, most)),
             dma((nd,)), dma((nd,)), dma((nd,)), dma((nd,)),
         ],
         compiler_params=pltpu.CompilerParams(

time: 28.1 us -> 28.7 us (1.021)
  Pallas kernels: 27.3 us -> 27.9 us
    pallas_call x1, Pallas kernels: 25.1 us -> 25.7 us  [exchange(): pl.pallas_call(functools.partial(exchange_kernel, nb, nd), out_shape=[jax...]
where the time goes in v4:
time: 28.7 us; the launch traced here: 28.5 us
  Pallas kernels  27.9 us (97%)
  between operations  0.64 us (2%)
    pallas_call x1, Pallas kernels, exchange(): pl.pallas_call(functools.partial(exchange_kernel, nb, nd), out_shape=[jax...  25.7 us
    pallas_call x1, Pallas kernels, write_descent(): pl.pallas_call(functools.partial(descent_kernel, nd), out_shape=[jax.Shap...  2.2 us

profile of v4, /device:TPU:0, one launch (start us, length us, event | category | flops | bytes accessed | tf_op | source)
XLA Modules:
  0.0 28.5 jit_solution(12711118636989048009)
XLA Ops:
  0.6 25.7 %exchange.1 = (f32[32,128,256]{2,1,0:T(8,128)S(1)}, f32[128,256]{1,0:T(8,128)S(1)}, f32[32,256]{1,0:T(8,128)S(1)}) custom-call(f32[32,128,256]{2,1,0:T(8,128)} %c_hbm.1, f32[128,256]{1,0:T(8,128)} %entry_hbm.1, f32[1,256]{1,0:T(1,128)} %bitcast.1, f32[5]{0:T(128)} %taps_hbm.1, f32[32,256]{1,0:T(8,128)} %measured_hbm.1), custom_call_target="tpu_custom_call" | custom-call | tf_op jit(solution)/shard_map/exchange/pallas_call | solution.py:463
  26.3 2.2 %descent.1 = (f32[32,128,256]{2,1,0:T(8,128)}, f32[32,32]{1,0:T(8,128)}) custom-call(f32[32,128,256]{2,1,0:T(8,128)S(1)} %get-tuple-element.5.part_ref, f32[128,256]{1,0:T(8,128)S(1)} %get-tuple-element.6.later_ref, f32[32,256]{1,0:T(8,128)S(1)} %get-tuple-element.7.res_ref), custom_call_target="tpu_custom_call" | custom-call | tf_op jit(solution)/shard_map/descent/pallas_call | solution.py:537

commit v5 on v4

--- a/solution.py
+++ b/solution.py
@@ -9,8 +9,8 @@
 
 MESH = pl.DeviceIdType.MESH
 ROWS, LANES = 8, 128
-SUBS = (2, 4)
-DIRECT = (0, 2)
+SUBS = (2, 2)
+DIRECT = (0, 0)
 WRITES = 8
 
 
@@ -235,9 +235,12 @@
         def _():
             result[rows, :] = jnp.zeros((half, height), jnp.float32)
 
+    def from_cores(ph, result):
+        to_partner(ph, 1).wait_recv()
+        from_core(ph, 0, result)
+        from_core(ph, 1, result)
+
     def finish_own(ph, result):
-        from_core(ph, 0, result)
-
         def body():
             for s in range(SUBS[ph]):
                 if s >= relayed[ph]:
@@ -248,9 +251,6 @@
         when_upstream(ph, body)
 
     def finish_other(ph, result):
-        to_partner(ph, 1).wait_recv()
-        from_core(ph, 1, result)
-
         def body():
             for s in range(SUBS[ph]):
                 rows = at(ph, other_start, s)
@@ -291,39 +291,64 @@
     for copy in small:
         copy.wait()
 
-    def weigh(i, carry):
-        rows = pl.ds(pl.multiple_of(i * ROWS, ROWS), ROWS)
-        for j in range(lane_blocks):
-            lanes = pl.ds(j * LANES, LANES)
-            rate = -absorb[:, lanes]
-            prior = w[0, rows, lanes]
-            part[0, rows, lanes] = prior
-            for b in range(1, cells):
-                c = w[b, rows, lanes]
-                part[b, rows, lanes] = c * jnp.exp(rate * prior)
-                prior = prior + c
-        return carry
-
-    def emit(g, carry):
-        for j in range(lane_blocks):
-            lanes = pl.ds(j * LANES, LANES)
-            sums = []
-            for r in range(ROWS):
-                acc = [None, None]
-                for t in range(tiles):
-                    rows = pl.ds(t * ROWS, ROWS)
-                    term = light[rows, lanes] * part[g * ROWS + r, rows, lanes]
-                    acc[t % 2] = term if acc[t % 2] is None else acc[t % 2] + term
-                sums.append(jnp.sum(acc[0] + acc[1], axis=0, keepdims=True))
-            img[g * lane_blocks + j] = jnp.concatenate(sums, axis=0)
-        return carry
-
-    lax.fori_loop(0, tiles, weigh, 0)
+    def weigh(start, first, last):
+        def tile(i, carry):
+            rows = pl.ds(pl.multiple_of(start + i * ROWS, ROWS), ROWS)
+            for j in range(lane_blocks):
+                lanes = pl.ds(j * LANES, LANES)
+                rate = -absorb[:, lanes]
+                prior = w[0, rows, lanes]
+                part[0, rows, lanes] = prior
+                for b in range(1, cells):
+                    c = w[b, rows, lanes]
+                    part[b, rows, lanes] = c * jnp.exp(rate * prior)
+                    prior = prior + c
+            return carry
+
+        lax.fori_loop(first, last, tile, 0)
+
+    def enter(rows):
+        light[rows, :] = entry[rows, :] * jnp.exp(-absorb[...] * before[rows, :])
+
+    def emit(start, last):
+        def group(g, carry):
+            for j in range(lane_blocks):
+                lanes = pl.ds(j * LANES, LANES)
+                tile_rows = [
+                    pl.ds(pl.multiple_of(start + t * ROWS, ROWS), ROWS)
+                    for t in range(half // ROWS)
+                ]
+                lamps = [light[rows, lanes] for rows in tile_rows]
+                sums = []
+                for r in range(ROWS):
+                    b = g * ROWS + r
+                    acc = [wide[b, :, lanes] if last else None, None]
+                    for t, rows in enumerate(tile_rows):
+                        term = lamps[t] * part[b, rows, lanes]
+                        acc[t % 2] = term if acc[t % 2] is None else acc[t % 2] + term
+                    total = acc[0] + acc[1]
+                    if last:
+                        sums.append(jnp.sum(total, axis=0, keepdims=True))
+                    else:
+                        wide[b, :, lanes] = total
+                if last:
+                    img[g * lane_blocks + j] = jnp.concatenate(sums, axis=0)
+            return carry
+
+        lax.fori_loop(0, cells // ROWS, group, 0)
+
+    half_tiles = half // ROWS
+    weigh(own_start, 0, half_tiles)
+    weigh(other_start, 0, half_tiles // 2)
+    from_cores(0, before)
     relay(0)
+    weigh(other_start, half_tiles // 2, half_tiles)
     finish_own(0, before)
+    enter(own_rows)
+    emit(own_start, False)
     finish_other(0, before)
-    light[...] = entry[...] * jnp.exp(-absorb[...] * before[...])
-    lax.fori_loop(0, cells // ROWS, emit, 0)
+    enter(other_rows)
+    emit(other_start, True)
 
     def guarded(index, body):
         if owners == nd:
@@ -429,10 +454,12 @@
         return carry
 
     lax.fori_loop(0, tiles, adjoint, 0)
+    from_cores(1, before)
     relay(1)
     finish_own(1, before)
+    later_out[own_rows, :] = absorb[...] * before[own_rows, :]
     finish_other(1, before)
-    later_out[...] = absorb[...] * before[...]
+    later_out[other_rows, :] = absorb[...] * before[other_rows, :]
 
     exchange_sent(0)
     exchange_sent(1)

time: 28.7 us -> 28.2 us (0.983)
  Pallas kernels: 27.9 us -> 27.5 us
    pallas_call x1, Pallas kernels: 25.7 us -> 25.3 us  [exchange(): pl.pallas_call(functools.partial(exchange_kernel, nb, nd), out_shape=[jax...]
where the time goes in v5:
time: 28.2 us; the launch traced here: 28.1 us
  Pallas kernels  27.5 us (98%)
  between operations  0.64 us (2%)
    pallas_call x1, Pallas kernels, exchange(): pl.pallas_call(functools.partial(exchange_kernel, nb, nd), out_shape=[jax...  25.3 us
    pallas_call x1, Pallas kernels, write_descent(): pl.pallas_call(functools.partial(descent_kernel, nd), out_shape=[jax.Shap...  2.2 us

profile of v5, /device:TPU:0, one launch (start us, length us, event | category | flops | bytes accessed | tf_op | source)
XLA Modules:
  0.0 28.1 jit_solution(18306968222111124704)
XLA Ops:
  0.6 25.3 %exchange.1 = (f32[32,128,256]{2,1,0:T(8,128)S(1)}, f32[128,256]{1,0:T(8,128)S(1)}, f32[32,256]{1,0:T(8,128)S(1)}) custom-call(f32[32,128,256]{2,1,0:T(8,128)} %c_hbm.1, f32[128,256]{1,0:T(8,128)} %entry_hbm.1, f32[1,256]{1,0:T(1,128)} %bitcast.1, f32[5]{0:T(128)} %taps_hbm.1, f32[32,256]{1,0:T(8,128)} %measured_hbm.1), custom_call_target="tpu_custom_call" | custom-call | tf_op jit(solution)/shard_map/exchange/pallas_call | solution.py:490
  25.9 2.2 %descent.1 = (f32[32,128,256]{2,1,0:T(8,128)}, f32[32,32]{1,0:T(8,128)}) custom-call(f32[32,128,256]{2,1,0:T(8,128)S(1)} %get-tuple-element.5.part_ref, f32[128,256]{1,0:T(8,128)S(1)} %get-tuple-element.6.later_ref, f32[32,256]{1,0:T(8,128)S(1)} %get-tuple-element.7.res_ref), custom_call_target="tpu_custom_call" | custom-call | tf_op jit(solution)/shard_map/descent/pallas_call | solution.py:564
